TPU v7x, 32 devices: a whole 2x2x4 slice. The times are simulated.
32 devices in a mesh: ap: 8 (over y, x, core), pass: 4 (over z).
Axes of the slice: x: 2, y: 2, z: 4, core: 2. Of those that a mesh axis runs over, the one named last changes fastest.
Arguments:
- echo: bfloat16 [4, 64, 2, 3072], P('pass', 'ap'), may hold values from -6 to 6
- chirp: bfloat16 [2, 1024], replicated, may hold values from -0.125 to 0.125
- pair_swap: int32 [4, 6], P('pass'), may hold values from 0 to 1
- range_shift: int32 [4, 6, 2], P('pass'), may hold values from -16 to 16, as said below
- angle_shift: int32 [4, 6, 2, 2], P('pass'), may hold values from -3 to 3, as said below
- range_taps: float32 [6, 2, 8], replicated, may hold values from -2 to 2
- angle_taps: float32 [6, 2, 2, 8], replicated, may hold values from -2 to 2
- phase_rates: float32 [6, 2, 2, 2], replicated, may hold values from -3.140625 to 3.140625
- invert: float32 [2, 64, 32], replicated, may hold values from -2 to 2
- baseline_index: int32 [4], replicated, may hold values from 0 to 31
Outputs:
- tomogram: float32 [4, 64, 8, 4096], P('pass', None, 'ap')
Inputs may be any that keep to these rules, and one draw needn't show every extreme that they name: `range_shift`: both 16 and -16 occur. `angle_shift`: both 3 and -3 occur.
All inputs are finite; a program needn't handle non-finite values.
Results may differ from a plain program's by a relative error of at most 0.0003.
Values sent between devices are 32-bit elements; how exact they have to be, the bound alone decides.
A program may use at most 64 MiB of HBM per device.

v0:
```python
import functools
import math

import jax
import jax.numpy as jnp
from jax import lax
from jax.experimental import pallas as pl
from jax.experimental.pallas import tpu as pltpu
from jax.sharding import PartitionSpec as P

RMAX = 16
PAD = 24
F32 = jnp.float32
BF16 = jnp.bfloat16
MESH = pl.DeviceIdType.MESH
LANES = 128


def up(value, unit):
    return -(-value // unit) * unit


def lane_iota(rows, lanes):
    return lax.broadcasted_iota(jnp.int32, (rows, lanes), 1)


def row_iota(rows, lanes):
    return lax.broadcasted_iota(jnp.int32, (rows, lanes), 0)


def sincos(theta):
    turns = jnp.floor(theta * (2.0 / math.pi) + 0.5)
    rest = theta - turns * 1.5703125
    rest = rest - turns * 4.837512969970703125e-4
    rest = rest - turns * 7.549789948768648e-8
    sq = rest * rest
    sine = rest + rest * sq * (
        -1.6666654611e-1 + sq * (8.3321608736e-3 + sq * -1.9515295891e-4)
    )
    cosine = 1.0 - 0.5 * sq + sq * sq * (
        4.166664568298827e-2 + sq * (-1.388731625493765e-3 + sq * 2.443315711809948e-5)
    )
    quadrant = turns.astype(jnp.int32) & 3
    odd = (quadrant & 1) == 1
    sin_out = jnp.where(odd, cosine, sine)
    cos_out = jnp.where(odd, sine, cosine)
    sin_out = jnp.where(quadrant >= 2, -sin_out, sin_out)
    cos_out = jnp.where((quadrant == 1) | (quadrant == 2), -cos_out, cos_out)
    return sin_out, cos_out


def take(ref, begin, rows, stride=None):
    where = pl.ds(begin, rows) if stride is None else pl.ds(begin, rows, stride=stride)
    return jnp.concatenate([ref[k, where, :] for k in range(ref.shape[0])], 1)


def put(ref, begin, value):
    for k in range(ref.shape[0]):
        ref[k, begin : begin + value.shape[0]] = value[:, k * LANES : (k + 1) * LANES]


def split(value):
    high = value.astype(BF16)
    low = (value - high.astype(F32)).astype(BF16)
    return high, low


def roles(swap_ref, level):
    swap = swap_ref[0, level]
    return [swap, 1 - swap]


def beam_matrix(level, beams, lanes, role, angle_shift, angle_taps):
    out_lane = lane_iota(8, lanes)[:1]
    q = out_lane & (2 * beams - 1)
    h_odd = (q & 1) == 1
    j_out = q >> 1
    core_rows = max(8, beams)
    j_in = row_iota(core_rows, lanes) & (beams - 1)
    in_row = row_iota(lanes, lanes)
    out_col = lane_iota(lanes, lanes)
    log_beams = beams.bit_length() - 1
    group_in = in_row >> (log_beams + 1)
    part_in = (in_row >> log_beams) & 1
    group_out = out_col >> (log_beams + 2)
    part_out = (out_col >> (log_beams + 1)) & 1
    same_part = part_in == part_out
    plain, turned = [], []
    for c in range(2):
        e = role[c]
        taps_count = angle_taps.shape[3]
        offset = jnp.where(
            h_odd, angle_shift[0, e, 1, level], angle_shift[0, e, 0, level]
        ) - (taps_count // 2 - 1)
        core = jnp.zeros((core_rows, lanes), F32)
        for u in range(taps_count):
            source = jnp.clip(j_out + offset + u, 0, beams - 1)
            weight = jnp.where(
                h_odd, angle_taps[level, e, 1, u], angle_taps[level, e, 0, u]
            ) * math.sqrt(0.5)
            core = core + jnp.where(j_in == source, weight, 0.0)
        full = jnp.concatenate([core] * (lanes // core_rows), 0)
        full = jnp.where(group_in == 2 * group_out + c, full, 0.0)
        plain.append(jnp.where(same_part, full, 0.0))
        turned.append(
            jnp.where(same_part, 0.0, jnp.where(part_out == 0, -full, full))
        )
    high, low = split(jnp.concatenate(plain + turned, 1))
    return jnp.concatenate([high, high, low], 0)


def phase_tables(level, beams, lanes, role, rates, origin, cells, count):
    q = lane_iota(8, lanes)[:1] & (2 * beams - 1)
    h_odd = (q & 1) == 1
    beam_at = q.astype(F32) * (1.0 / (2 * beams))
    row = row_iota(8, lanes)
    tiles = count // 8
    doublings = max(tiles - 1, 1).bit_length()
    tables = []
    for c in range(2):
        e = role[c]
        slope = jnp.where(h_odd, rates[e, 1, 0, level], rates[e, 0, 0, level]) * (8.0 / cells)
        tilt = jnp.where(h_odd, rates[e, 1, 1, level], rates[e, 0, 1, level]) * 8.0
        first = slope * (origin + row).astype(F32) + tilt * beam_at
        steps = slope * (8 << row).astype(F32)
        sines, cosines = sincos(jnp.concatenate([first, steps], 0))
        sin_tiles, cos_tiles = [sines[:8]], [cosines[:8]]
        for m in range(doublings):
            s_step, c_step = sines[8 + m : 9 + m], cosines[8 + m : 9 + m]
            for a in range(1 << m):
                if len(sin_tiles) < tiles:
                    s_old, c_old = sin_tiles[a], cos_tiles[a]
                    sin_tiles.append(s_old * c_step + c_old * s_step)
                    cos_tiles.append(c_old * c_step - s_old * s_step)
        tables.append((jnp.concatenate(cos_tiles, 0), jnp.concatenate(sin_tiles, 0)))
    return tables


def merge(level, beams, lo, hi, src, z_ref, params, origin, cells):
    swap_ref, range_shift, angle_shift, range_taps, angle_taps, rates = params
    lanes = src.shape[0] * LANES
    rows = hi - lo
    role = roles(swap_ref, level)
    child = (lane_iota(8, lanes)[:1] >> beams.bit_length()) & 1
    taps_count = range_taps.shape[2]
    o = taps_count // 2 - 1
    starts = [PAD + lo - o + range_shift[0, e, level] for e in role]
    aligned = jnp.where(
        child == 0, take(src, starts[0], rows + 8), take(src, starts[1], rows + 8)
    )
    put(z_ref, 0, aligned)
    ranged = jnp.zeros((rows, lanes), F32)
    for t in range(taps_count):
        weight = jnp.where(
            child == 0, range_taps[level, role[0], t], range_taps[level, role[1], t]
        )
        ranged = ranged + weight * take(z_ref, t, rows)
    high, low = split(ranged)
    weights = beam_matrix(level, beams, lanes, role, angle_shift, angle_taps)
    product = jnp.dot(
        jnp.concatenate([high, low, high], 1), weights, preferred_element_type=F32
    )
    (cos0, sin0), (cos1, sin1) = phase_tables(
        level, beams, lanes, role, rates, origin + lo, cells, rows
    )
    return (
        cos0 * product[:, :lanes]
        + cos1 * product[:, lanes : 2 * lanes]
        + sin0 * product[:, 2 * lanes : 3 * lanes]
        + sin1 * product[:, 3 * lanes :]
    )


def image_kernel(
    sizes,
    echo,
    chirp,
    swap_ref,
    range_shift,
    angle_shift,
    range_taps,
    angle_taps,
    rates,
    out,
    echo_rows,
    chirp_rows,
    image_a,
    image_b,
    z_ref,
    send_ap,
    recv_ap,
    send_pass,
    send_sem,
    recv_sem,
    send_sem2,
    recv_sem2,
):
    n, passes, pulses, cells, levels = sizes
    lanes = n * 2 * pulses
    taps_count = chirp.shape[1]
    samples = echo.shape[3]
    block = cells // n
    reach = RMAX + range_taps.shape[2] // 2
    local = pulses.bit_length() - 1
    cross = levels - local
    wide = up(block + 2 * reach * cross, LANES)
    halo = (wide - block) // 2
    rim = up(reach * local, 64)
    window = wide + 2 * rim
    start = halo + rim
    me = lax.axis_index("ap")
    my_pass = lax.axis_index("pass")
    params = (swap_ref, range_shift, angle_shift, range_taps, angle_taps, rates)

    def rev(index):
        total = 0
        for digit in range(cross):
            total = total + (index // 2**digit) % 2 * 2 ** (cross - 1 - digit)
        return total

    barrier = pltpu.get_barrier_semaphore()
    for i in range(1, n):
        pl.semaphore_signal(
            barrier, inc=1, device_id=(lax.rem(me + i, n), my_pass), device_id_type=MESH
        )
    for i in range(1, passes):
        pl.semaphore_signal(
            barrier, inc=1, device_id=(me, lax.rem(my_pass + i, passes)), device_id_type=MESH
        )

    depth = up(block + taps_count - 1, LANES)
    for pulse in range(pulses):
        echo_rows[2 * pulse : 2 * pulse + 2, :samples] = echo[0, pulse].astype(F32)
    need = block * (n - 1) + depth
    if need > samples:
        echo_rows[:, samples:] = jnp.zeros((2 * pulses, echo_rows.shape[1] - samples), F32)
    echo_cat = jnp.concatenate(
        [echo_rows[:, k * block : k * block + depth].astype(BF16) for k in range(n)], 0
    )
    taps = chirp[...].astype(F32)
    sub = row_iota(8, depth)
    for part in range(2):
        wide_row = jnp.concatenate(
            [
                jnp.broadcast_to(taps[part : part + 1], (8, taps_count)),
                jnp.zeros((8, depth - taps_count), F32),
            ],
            1,
        )
        base = wide_row
        for s in range(1, 8):
            base = jnp.where(sub == s, pltpu.roll(wide_row, s, 1), base)
        for a in range(0, min(block, LANES), 16):
            pair = [base if a == 0 else pltpu.roll(base, a, 1), pltpu.roll(base, a + 8, 1)]
            rows16 = jnp.concatenate(pair, 0).astype(BF16)
            for b in range(max(block // LANES, 1)):
                if b:
                    rows16 = jnp.concatenate([rows16[:, -LANES:], rows16[:, :-LANES]], 1)
                at = part * block + b * LANES + a
                chirp_rows[at : at + 16, :] = rows16
    product = lax.dot_general(
        chirp_rows[...], echo_cat, (((1,), (1,)), ((), ())), preferred_element_type=F32
    )
    crossed = product[block:]
    odd = (lane_iota(8, lanes)[:1] & 1) == 1
    compressed = product[:block] + jnp.where(
        odd, -pltpu.roll(crossed, 1, 1), pltpu.roll(crossed, lanes - 1, 1)
    )

    per = 2 * pulses
    lane_block = lane_iota(8, lanes)[:1] >> (per.bit_length() - 1)

    def pieces(lo, hi):
        at = lo
        while at < hi:
            q = (at - start) // block
            end = min(hi, start + (q + 1) * block)
            yield at, end, q
            at = end

    def keep(q):
        return (lane_block + q >= 0) & (lane_block + q < n)

    blank = jnp.zeros((PAD + 24, lanes), F32)
    put(image_a, 0, blank[:PAD])
    put(image_b, 0, blank)
    put(image_a, PAD + window, blank[:PAD])
    put(image_b, PAD + window - 24, blank)
    for at, end, q in pieces(0, window):
        from_row = at - start - q * block
        piece = compressed[from_row : from_row + end - at]
        if q:
            piece = jnp.where(keep(q), pltpu.roll(piece, (-q * per) % lanes, 1), 0.0)
        put(image_a, PAD + at, piece)

    origin = lane_block * block - start
    src, dst = image_a, image_b
    for level in range(local):
        margin = (level + 1) * reach // 8 * 8 if level + 1 < local else rim
        merged = merge(
            level, 2**level, margin, window - margin, src, z_ref, params, origin, cells
        )
        masked = []
        for at, end, q in pieces(margin, window - margin):
            piece = merged[at - margin : end - margin]
            masked.append(jnp.where(keep(q), piece, 0.0) if q else piece)
        merged = jnp.concatenate(masked, 0)
        if level + 1 < local:
            put(dst, PAD + margin, merged)
            src, dst = dst, src
    send_ap[...] = merged.T.reshape(n, per, wide)

    pl.semaphore_wait(barrier, n - 1 + passes - 1)
    copies = []
    for i in range(1, n):
        to = lax.rem(me + i, n)
        copy = pltpu.make_async_remote_copy(
            src_ref=send_ap.at[rev(to)],
            dst_ref=recv_ap.at[me],
            send_sem=send_sem.at[i],
            recv_sem=recv_sem.at[i],
            device_id=(to, my_pass),
            device_id_type=MESH,
        )
        copy.start()
        copies.append(copy)
    recv_ap[me] = send_ap[rev(me)]
    for copy in copies:
        copy.wait()
    put(image_a, PAD, recv_ap[...].reshape(lanes, wide).T)
    put(image_a, PAD + wide, blank[:PAD])
    put(image_b, PAD + wide - 24, blank)

    origin = rev(me) * block - halo
    src, dst = image_a, image_b
    for digit in range(cross):
        level = local + digit
        last = digit + 1 == cross
        margin = halo if last else (digit + 1) * reach // 8 * 8
        merged = merge(
            level, 2**level, margin, wide - margin, src, z_ref, params, origin, cells
        )
        if not last:
            at = origin + margin + row_iota(wide - 2 * margin, lanes)
            merged = jnp.where((at >= 0) & (at < cells), merged, 0.0)
        put(dst, PAD + margin, merged)
        src, dst = dst, src

    beams = 2**levels
    share = beams // passes
    spread = LANES // share
    count = block // spread
    group = lane_iota(8, LANES)[:1] >> (share.bit_length() - 1)
    rows = [take(src, PAD + halo + s, count, spread) for s in range(spread)]
    for b in range(passes):
        for c in range(2):
            lane = c * beams + b * share
            base, inner = lane // LANES * LANES, lane % LANES
            gathered = None
            for s in range(spread):
                moved = pltpu.roll(
                    rows[s][:, base : base + LANES], (s * share - inner) % LANES, 1
                )
                gathered = moved if s == 0 else jnp.where(group == s, moved, gathered)
            send_pass[b, c * count : (c + 1) * count] = gathered
    copies = []
    for i in range(1, passes):
        to = lax.rem(my_pass + i, passes)
        copy = pltpu.make_async_remote_copy(
            src_ref=send_pass.at[to],
            dst_ref=out.at[my_pass],
            send_sem=send_sem2.at[i],
            recv_sem=recv_sem2.at[i],
            device_id=(me, to),
            device_id_type=MESH,
        )
        copy.start()
        copies.append(copy)
    out[my_pass] = send_pass[my_pass]
    for copy in copies:
        copy.wait()


def power_kernel(passes, count, data, invert, baseline, out):
    bases, heights = invert.shape[1], invert.shape[2]
    real, imag = invert[0], invert[1]
    table = jnp.concatenate(
        [jnp.concatenate([real, imag], 1), jnp.concatenate([-imag, real], 1)], 0
    ).T
    table_high, table_low = split(table)
    row = row_iota(2 * bases, 2 * passes)
    column = lane_iota(2 * bases, 2 * passes)
    chosen = jnp.zeros((2 * bases, 2 * passes), F32)
    for p in range(passes):
        for c in range(2):
            hit = (column == 2 * p + c) & (row == c * bases + baseline[p])
            chosen = jnp.where(hit, 1.0, chosen)
    chosen = chosen.astype(BF16)
    mixer_high = jnp.dot(table_high, chosen, preferred_element_type=F32).astype(BF16)
    mixer_low = jnp.dot(table_low, chosen, preferred_element_type=F32).astype(BF16)
    mixer = jnp.concatenate([mixer_high, mixer_high, mixer_low], 1)
    chunk = min(count, 8)
    for a0 in range(0, count, chunk):
        values = jnp.concatenate(
            [data[pl.ds(a, 2 * passes, stride=count), :] for a in range(a0, a0 + chunk)], 1
        )
        high = values.astype(BF16).astype(F32)
        low = values - high
        stack = jnp.concatenate([high, low, high], 0).astype(BF16)
        tomo = jnp.dot(mixer, stack, preferred_element_type=F32)
        power = tomo[:heights] * tomo[:heights] + tomo[heights:] * tomo[heights:]
        for a in range(chunk):
            out[pl.ds(a0 + a, heights, stride=count), :] = power[:, a * LANES : (a + 1) * LANES]


def body(
    mesh_shape,
    echo,
    chirp,
    pair_swap,
    range_shift,
    angle_shift,
    range_taps,
    angle_taps,
    phase_rates,
    invert,
    baseline_index,
):
    n, passes = mesh_shape["ap"], mesh_shape["pass"]
    pulses, samples = echo.shape[1], echo.shape[3]
    levels = range_taps.shape[0]
    taps_count = chirp.shape[1]
    cells = samples - taps_count
    block = cells // n
    beams = 2**levels
    share = beams // passes
    heights = invert.shape[1]
    count = block * share // LANES
    lanes = n * 2 * pulses
    reach = RMAX + range_taps.shape[2] // 2
    local = pulses.bit_length() - 1
    wide = up(block + 2 * reach * (levels - local), LANES)
    window = wide + 2 * up(reach * local, 64)
    depth = up(block + taps_count - 1, LANES)
    vmem = pl.BlockSpec(memory_space=pltpu.VMEM)
    smem = pl.BlockSpec(memory_space=pltpu.SMEM)
    stacks = pl.pallas_call(
        functools.partial(image_kernel, (n, passes, pulses, cells, levels)),
        out_shape=jax.ShapeDtypeStruct((passes, 2 * count, LANES), F32),
        in_specs=[vmem] * 2 + [smem] * 6,
        out_specs=vmem,
        scratch_shapes=[
            pltpu.VMEM((2 * pulses, up(max(samples, block * (n - 1) + depth), LANES)), F32),
            pltpu.VMEM((2 * block, depth), BF16),
            pltpu.VMEM((lanes // LANES, window + 2 * PAD, LANES), F32),
            pltpu.VMEM((lanes // LANES, window + 2 * PAD, LANES), F32),
            pltpu.VMEM((lanes // LANES, window, LANES), F32),
            pltpu.VMEM((n, 2 * pulses, wide), F32),
            pltpu.VMEM((n, 2 * pulses, wide), F32),
            pltpu.VMEM((passes, 2 * count, LANES), F32),
            pltpu.SemaphoreType.DMA((n,)),
            pltpu.SemaphoreType.DMA((n,)),
            pltpu.SemaphoreType.DMA((passes,)),
            pltpu.SemaphoreType.DMA((passes,)),
        ],
        compiler_params=pltpu.CompilerParams(
            collective_id=0, has_side_effects=True, vmem_limit_bytes=48 * 2**20
        ),
        name="image",
    )(
        echo,
        chirp,
        pair_swap,
        jnp.transpose(range_shift, (0, 2, 1)),
        jnp.transpose(angle_shift, (0, 2, 3, 1)),
        range_taps,
        angle_taps,
        jnp.transpose(phase_rates, (1, 2, 3, 0)),
    )
    power = pl.pallas_call(
        functools.partial(power_kernel, passes, count),
        out_shape=jax.ShapeDtypeStruct((heights * count, LANES), F32),
        in_specs=[vmem, vmem, smem],
        out_specs=vmem,
        compiler_params=pltpu.CompilerParams(vmem_limit_bytes=32 * 2**20),
        name="power",
    )(
        stacks.reshape(passes * 2 * count, LANES),
        jnp.transpose(invert, (0, 2, 1)),
        baseline_index,
    )
    return power.reshape(1, heights, 1, block * share)


def solution(mesh):
    return jax.shard_map(
        functools.partial(body, dict(mesh.shape)),
        mesh=mesh,
        in_specs=(
            P("pass", "ap", None, None),
            P(),
            P("pass", None),
            P("pass", None, None),
            P("pass", None, None, None),
            P(),
            P(),
            P(),
            P(),
            P(),
        ),
        out_specs=P("pass", None, "ap", None),
        check_vma=False,
    )
```

profile of v0, /device:TPU:0, one launch (start us, length us, event | category | flops | bytes accessed | tf_op | source)
XLA Modules:
  0.0 25.7 jit_solution(11336135213758384468)
XLA Ops:
  0.0 0.0 copy-start.3
  0.0 0.0 copy-start.7
  0.0 0.0 copy-start.8
  0.0 0.7 %copy-done.3 = f32[6,2,8]{2,1,0:T(2,128)S(1)} copy-done((f32[6,2,8]{2,1,0:T(2,128)S(1)}, f32[6,2,8]{2,1,0:T(2,128)}, u32[]{:S(2)}) %copy-start.3) | copy-done | bytes 408
  0.7 0.0 copy-done.7
  0.7 0.0 copy-done.8
  0.7 0.0 copy-start
  0.7 0.9 %copy-done = bf16[1,8,2,3072]{3,2,1,0:T(2,128)(2,1)S(1)} copy-done((bf16[1,8,2,3072]{3,2,1,0:T(2,128)(2,1)S(1)}, bf16[1,8,2,3072]{3,2,1,0:T(2,128)(2,1)}, u32[]{:S(2)}) %copy-start) | copy-done | bytes 98328
  1.6 0.0 copy-start.2
  1.6 0.7 %copy-done.2 = f32[6,2,2,8]{3,2,1,0:T(2,128)S(1)} copy-done((f32[6,2,2,8]{3,2,1,0:T(2,128)S(1)}, f32[6,2,2,8]{3,2,1,0:T(2,128)}, u32[]{:S(2)}) %copy-start.2) | copy-done | bytes 792
  2.3 0.0 copy-start.4
  2.3 0.7 %copy-done.4 = bf16[2,1024]{1,0:T(2,128)(2,1)S(1)} copy-done((bf16[2,1024]{1,0:T(2,128)(2,1)S(1)}, bf16[2,1024]{1,0:T(2,128)(2,1)}, u32[]{:S(2)}) %copy-start.4) | copy-done | bytes 4120
  3.0 0.0 copy-start.5
  3.0 0.7 %copy-done.5 = f32[6,2,2,2]{0,3,2,1:T(2,128)S(1)} copy-done((f32[6,2,2,2]{0,3,2,1:T(2,128)S(1)}, f32[6,2,2,2]{0,3,2,1:T(2,128)}, u32[]{:S(2)}) %copy-start.5) | copy-done | bytes 216
  3.7 0.0 copy-start.6
  3.7 0.7 %copy-done.6 = s32[1,6,2,2]{1,3,2,0:T(2,128)S(1)} copy-done((s32[1,6,2,2]{1,3,2,0:T(2,128)S(1)}, s32[1,6,2,2]{1,3,2,0:T(2,128)}, u32[]{:S(2)}) %copy-start.6) | copy-done | bytes 120
  4.4 0.0 copy-start.1
  4.4 18.0 %image.1 = f32[4,64,128]{2,1,0:T(8,128)S(1)} custom-call(bf16[1,8,2,3072]{3,2,1,0:T(2,128)(2,1)S(1)} %copy-done, bf16[2,1024]{1,0:T(2,128)(2,1)S(1)} %copy-done.4, s32[1,6]{1,0:T(1,128)S(1)} %copy-done.8, s32[1,2,6]{2,1,0:T(2,128)S(1)} %bitcast.10, s32[1,2,2,6]{3,2,1,0:T(2,128)S(1)} %bitcast.9, f32[6,2,8]{2,1,0:T(2,128)S(1)} %copy-done.3, ...), custom_call_target="tpu_custom_call" | custom-call | tf_op jit(solution)/shard_map/image/pallas_call | solution.py:447
  22.4 0.0 copy-start.9
  22.4 0.0 copy-done.1
  22.4 0.6 %copy-done.9 = s32[4]{0:T(128)S(1)} copy-done((s32[4]{0:T(128)S(1)}, s32[4]{0:T(128)}, u32[]{:S(2)}) %copy-start.9) | copy-done | bytes 40
  23.0 2.7 %power.1 = f32[2048,128]{1,0:T(8,128)} custom-call(f32[256,128]{1,0:T(8,128)S(1)} %bitcast.6, f32[2,32,64]{2,1,0:T(8,128)S(1)} %bitcast.7, s32[4]{0:T(128)S(1)} %copy-done.9), custom_call_target="tpu_custom_call" | custom-call | tf_op jit(solution)/shard_map/power/pallas_call | solution.py:480
Async XLA Ops:
  0.0 0.7 %copy-start.3 = (f32[6,2,8]{2,1,0:T(2,128)S(1)}, f32[6,2,8]{2,1,0:T(2,128)}, u32[]{:S(2)}) copy-start(f32[6,2,8]{2,1,0:T(2,128)} %range_taps.1) | copy-start | bytes 1156
  0.0 0.7 %copy-start.7 = (s32[1,6,2]{1,2,0:T(2,128)S(1)}, s32[1,6,2]{1,2,0:T(2,128)}, u32[]{:S(2)}) copy-start(s32[1,6,2]{1,2,0:T(2,128)} %param.13) | copy-start | bytes 148
  0.0 0.7 %copy-start.8 = (s32[1,6]{1,0:T(1,128)S(1)}, s32[1,6]{1,0:T(1,128)}, u32[]{:S(2)}) copy-start(s32[1,6]{1,0:T(1,128)} %swap_ref.1) | copy-start | bytes 76
  0.7 0.9 %copy-start = (bf16[1,8,2,3072]{3,2,1,0:T(2,128)(2,1)S(1)}, bf16[1,8,2,3072]{3,2,1,0:T(2,128)(2,1)}, u32[]{:S(2)}) copy-start(bf16[1,8,2,3072]{3,2,1,0:T(2,128)(2,1)} %echo.1) | copy-start | bytes 294916
  1.6 0.7 %copy-start.2 = (f32[6,2,2,8]{3,2,1,0:T(2,128)S(1)}, f32[6,2,2,8]{3,2,1,0:T(2,128)}, u32[]{:S(2)}) copy-start(f32[6,2,2,8]{3,2,1,0:T(2,128)} %angle_taps.1) | copy-start | bytes 2308
  2.3 0.7 %copy-start.4 = (bf16[2,1024]{1,0:T(2,128)(2,1)S(1)}, bf16[2,1024]{1,0:T(2,128)(2,1)}, u32[]{:S(2)}) copy-start(bf16[2,1024]{1,0:T(2,128)(2,1)} %chirp.1) | copy-start | bytes 12292
  3.0 0.7 %copy-start.5 = (f32[6,2,2,2]{0,3,2,1:T(2,128)S(1)}, f32[6,2,2,2]{0,3,2,1:T(2,128)}, u32[]{:S(2)}) copy-start(f32[6,2,2,2]{0,3,2,1:T(2,128)} %param.17) | copy-start | bytes 580
  3.7 0.7 %copy-start.6 = (s32[1,6,2,2]{1,3,2,0:T(2,128)S(1)}, s32[1,6,2,2]{1,3,2,0:T(2,128)}, u32[]{:S(2)}) copy-start(s32[1,6,2,2]{1,3,2,0:T(2,128)} %param.14) | copy-start | bytes 292
  4.4 18.0 %copy-start.1 = (f32[2,64,32]{1,2,0:T(8,128)S(1)}, f32[2,64,32]{1,2,0:T(8,128)}, u32[]{:S(2)}) copy-start(f32[2,64,32]{1,2,0:T(8,128)} %param.18) | copy-start | bytes 49156
  22.4 0.7 %copy-start.9 = (s32[4]{0:T(128)S(1)}, s32[4]{0:T(128)}, u32[]{:S(2)}) copy-start(s32[4]{0:T(128)} %baseline.1) | copy-start | bytes 52
where the time goes:
time: 26.1 us; the launch traced here: 25.7 us
  Pallas kernels  20.7 us (79%)
  local copies, waits for them, and re-layouts  4.99 us (19%)
    pallas_call x1, Pallas kernels, body(): pl.pallas_call(functools.partial(image_kernel, (n, passes, pulses, cells,...  18 us
    unnamed x20, local copies, waits for them, and re-layouts  4.99 us
    pallas_call x1, Pallas kernels, body(): pl.pallas_call(functools.partial(power_kernel, passes, count), out_shape=...  2.72 us

commit v1 on v0

v1 whole, which is shorter than its diff:
```python
import functools
import math

import jax
import jax.numpy as jnp
from jax import lax
from jax.experimental import pallas as pl
from jax.experimental.pallas import tpu as pltpu
from jax.sharding import PartitionSpec as P

RMAX = 16
PAD = 24
F32 = jnp.float32
BF16 = jnp.bfloat16
MESH = pl.DeviceIdType.MESH
LANES = 128


def up(value, unit):
    return -(-value // unit) * unit


def lane_iota(rows, lanes):
    return lax.broadcasted_iota(jnp.int32, (rows, lanes), 1)


def row_iota(rows, lanes):
    return lax.broadcasted_iota(jnp.int32, (rows, lanes), 0)


def sincos(theta):
    turns = jnp.floor(theta * (2.0 / math.pi) + 0.5)
    rest = theta - turns * 1.5703125
    rest = rest - turns * 4.837512969970703125e-4
    rest = rest - turns * 7.549789948768648e-8
    sq = rest * rest
    sine = rest + rest * sq * (
        -1.6666654611e-1 + sq * (8.3321608736e-3 + sq * -1.9515295891e-4)
    )
    cosine = 1.0 - 0.5 * sq + sq * sq * (
        4.166664568298827e-2 + sq * (-1.388731625493765e-3 + sq * 2.443315711809948e-5)
    )
    quadrant = turns.astype(jnp.int32) & 3
    odd = (quadrant & 1) == 1
    sin_out = jnp.where(odd, cosine, sine)
    cos_out = jnp.where(odd, sine, cosine)
    sin_out = jnp.where(quadrant >= 2, -sin_out, sin_out)
    cos_out = jnp.where((quadrant == 1) | (quadrant == 2), -cos_out, cos_out)
    return sin_out, cos_out


def take(ref, begin, rows, stride=None):
    where = pl.ds(begin, rows) if stride is None else pl.ds(begin, rows, stride=stride)
    return jnp.concatenate([ref[k, where, :] for k in range(ref.shape[0])], 1)


def put(ref, begin, value):
    for k in range(ref.shape[0]):
        ref[k, begin : begin + value.shape[0]] = value[:, k * LANES : (k + 1) * LANES]


def split(value):
    high = value.astype(BF16)
    low = (value - high.astype(F32)).astype(BF16)
    return high, low


def roles(swap_ref, level):
    swap = swap_ref[0, level]
    return [swap, 1 - swap]


def prepare(level, beams, origin, tiles, cells, params, w_ref, table_ref):
    swap_ref, _, angle_shift, _, angle_taps, rates = params
    lanes = w_ref.shape[2] // 4
    role = roles(swap_ref, level)
    taps_count = angle_taps.shape[3]
    q = lane_iota(8, lanes)[:1] & (2 * beams - 1)
    h_odd = (q & 1) == 1
    j_out = q >> 1
    log_beams = beams.bit_length() - 1
    part_out = (lane_iota(16, lanes) >> (log_beams + 1)) & 1
    group_out = lane_iota(16, lanes) >> (log_beams + 2)
    core_rows = max(16, beams)
    j_in = row_iota(core_rows, lanes) & (beams - 1)
    cores = []
    for e in role:
        offset = jnp.where(
            h_odd, angle_shift[0, e, 1, level], angle_shift[0, e, 0, level]
        ) - (taps_count // 2 - 1)
        core = jnp.zeros((core_rows, lanes), F32)
        for u in range(taps_count):
            source = jnp.clip(j_out + offset + u, 0, beams - 1)
            weight = jnp.where(
                h_odd, angle_taps[level, e, 1, u], angle_taps[level, e, 0, u]
            ) * math.sqrt(0.5)
            core = core + jnp.where(j_in == source, weight, 0.0)
        cores.append(core)
    for at in range(0, lanes, 16):
        in_row = at + row_iota(16, lanes)
        group_in = in_row >> (log_beams + 1)
        same_part = ((in_row >> log_beams) & 1) == part_out
        for c in range(2):
            core = cores[c][at % core_rows : at % core_rows + 16]
            full = jnp.where(group_in == 2 * group_out + c, core, 0.0)
            plain = jnp.where(same_part, full, 0.0)
            turned = jnp.where(same_part, 0.0, jnp.where(part_out == 0, -full, full))
            for place, value in ((c, plain), (2 + c, turned)):
                high, low = split(value)
                columns = slice(place * lanes, (place + 1) * lanes)
                w_ref[level, at : at + 16, columns] = high
                w_ref[level, lanes + at : lanes + at + 16, columns] = high
                w_ref[level, 2 * lanes + at : 2 * lanes + at + 16, columns] = low

    beam_at = q.astype(F32) * (1.0 / (2 * beams))
    row = row_iota(8, lanes)
    groups = -(-tiles // 8)
    for c, e in enumerate(role):
        slope = jnp.where(h_odd, rates[e, 1, 0, level], rates[e, 0, 0, level]) * (8.0 / cells)
        tilt = jnp.where(h_odd, rates[e, 1, 1, level], rates[e, 0, 1, level]) * 8.0
        first = slope * (origin + row).astype(F32) + tilt * beam_at
        along = slope * (8 * row).astype(F32)
        steps = slope * (64 << row).astype(F32)
        sines, cosines = sincos(jnp.concatenate([first, along, steps], 0))
        table_ref[level, c, 0, :8] = cosines[:8]
        table_ref[level, c, 1, :8] = sines[:8]
        held = [(cosines[8:16], sines[8:16])]
        m = 0
        while len(held) < groups:
            s_step, c_step = sines[16 + m : 17 + m], cosines[16 + m : 17 + m]
            for c_old, s_old in held[: groups - len(held)]:
                held.append((c_old * c_step - s_old * s_step, s_old * c_step + c_old * s_step))
            m += 1
        for k, (cosine, sine) in enumerate(held):
            table_ref[level, c, 0, 8 + 8 * k : 16 + 8 * k] = cosine
            table_ref[level, c, 1, 8 + 8 * k : 16 + 8 * k] = sine


def merge(level, beams, lo, hi, src, dst, valid, params, z_ref, x_ref, p_ref, w_ref, table_ref):
    swap_ref, range_shift, _, range_taps, _, _ = params
    lanes = src.shape[0] * LANES
    rows = hi - lo
    role = roles(swap_ref, level)
    child = (lane_iota(8, lanes)[:1] >> beams.bit_length()) & 1
    first = child == 0
    taps_count = range_taps.shape[2]
    o = taps_count // 2 - 1
    starts = [PAD + lo - o + range_shift[0, e, level] for e in role]
    for at in range(0, rows + 8, 64):
        n = min(64, rows + 8 - at)
        put(z_ref, at, jnp.where(first, take(src, starts[0] + at, n), take(src, starts[1] + at, n)))
    weights = [
        jnp.where(first, range_taps[level, role[0], t], range_taps[level, role[1], t])
        for t in range(taps_count)
    ]
    for at in range(0, rows, 32):
        n = min(32, rows - at)
        ranged = weights[0] * take(z_ref, at, n)
        for t in range(1, taps_count):
            ranged = ranged + weights[t] * take(z_ref, at + t, n)
        high, low = split(ranged)
        x_ref[at : at + n, :lanes] = high
        x_ref[at : at + n, lanes : 2 * lanes] = low
        x_ref[at : at + n, 2 * lanes :] = high
    p_ref[:rows] = jnp.dot(x_ref[:rows], w_ref[level], preferred_element_type=F32)
    base = [(table_ref[level, c, 0, :8], table_ref[level, c, 1, :8]) for c in range(2)]
    for a in range(rows // 8):
        total = None
        for c in range(2):
            c_step = table_ref[level, c, 0, 8 + a : 9 + a]
            s_step = table_ref[level, c, 1, 8 + a : 9 + a]
            c_base, s_base = base[c]
            cosine = c_base * c_step - s_base * s_step
            sine = s_base * c_step + c_base * s_step
            plain = p_ref[8 * a : 8 * a + 8, c * lanes : (c + 1) * lanes]
            turned = p_ref[8 * a : 8 * a + 8, (2 + c) * lanes : (3 + c) * lanes]
            term = cosine * plain + sine * turned
            total = term if c == 0 else total + term
        at = lo + 8 * a
        if valid is not None:
            origin, block, halo, cells = valid
            if at < halo or at >= halo + block:
                cell = origin + at + row_iota(8, lanes)
                total = jnp.where((cell >= 0) & (cell < cells), total, 0.0)
        put(dst, PAD + at, total)


def image_kernel(
    sizes,
    echo_in,
    chirp_in,
    swap_in,
    range_shift_in,
    angle_shift_in,
    range_taps_in,
    angle_taps_in,
    rates_in,
    invert_in,
    baseline_in,
    out,
    mixer,
    echo,
    chirp,
    swap_ref,
    range_shift,
    angle_shift,
    range_taps,
    angle_taps,
    rates,
    invert,
    baseline,
    echo_rows,
    chirp_rows,
    image_a,
    image_b,
    z_ref,
    x_ref,
    p_ref,
    w_ref,
    table_ref,
    send_ap,
    recv_ap,
    send_pass,
    in_sem,
    send_sem,
    recv_sem,
    send_sem2,
    recv_sem2,
):
    n, passes, pulses, cells, levels = sizes
    lanes = n * 2 * pulses
    taps_count = chirp.shape[1]
    samples = echo.shape[3]
    block = cells // n
    reach = RMAX + range_taps.shape[2] // 2
    local = pulses.bit_length() - 1
    cross = levels - local
    wide = up(block + 2 * reach * cross, LANES)
    halo = (wide - block) // 2
    me = lax.axis_index("ap")
    my_pass = lax.axis_index("pass")
    params = (swap_ref, range_shift, angle_shift, range_taps, angle_taps, rates)

    def rev(index):
        total = 0
        for digit in range(cross):
            total = total + (index // 2**digit) % 2 * 2 ** (cross - 1 - digit)
        return total

    pairs = [
        (swap_in, swap_ref),
        (angle_shift_in, angle_shift),
        (angle_taps_in, angle_taps),
        (rates_in, rates),
        (range_shift_in, range_shift),
        (range_taps_in, range_taps),
        (baseline_in, baseline),
        (chirp_in, chirp),
        (echo_in, echo),
        (invert_in, invert),
    ]
    fetches = [
        pltpu.make_async_copy(there, here, in_sem.at[i]) for i, (there, here) in enumerate(pairs)
    ]
    for fetch in fetches:
        fetch.start()

    barrier = pltpu.get_barrier_semaphore()
    for i in range(1, n):
        pl.semaphore_signal(
            barrier, inc=1, device_id=(lax.rem(me + i, n), my_pass), device_id_type=MESH
        )
    for i in range(1, passes):
        pl.semaphore_signal(
            barrier, inc=1, device_id=(me, lax.rem(my_pass + i, passes)), device_id_type=MESH
        )

    blank = jnp.zeros((PAD, lanes), F32)
    put(image_b, 0, blank)

    per = 2 * pulses
    lane_block = lane_iota(8, lanes)[:1] >> (per.bit_length() - 1)
    for fetch in fetches[:7]:
        fetch.wait()
    for level in range(local):
        prepare(
            level, 2**level, lane_block * block, block // 8, cells, params, w_ref, table_ref
        )

    fetches[7].wait()
    depth = up(block + taps_count - 1, LANES)
    taps = chirp[...].astype(F32)
    sub = row_iota(8, depth)
    for part in range(2):
        wide_row = jnp.concatenate(
            [
                jnp.broadcast_to(taps[part : part + 1], (8, taps_count)),
                jnp.zeros((8, depth - taps_count), F32),
            ],
            1,
        )
        base = wide_row
        for s in range(1, 8):
            base = jnp.where(sub == s, pltpu.roll(wide_row, s, 1), base)
        for a in range(0, min(block, LANES), 16):
            pair = [base if a == 0 else pltpu.roll(base, a, 1), pltpu.roll(base, a + 8, 1)]
            rows16 = jnp.concatenate(pair, 0).astype(BF16)
            for b in range(max(block // LANES, 1)):
                if b:
                    rows16 = jnp.concatenate([rows16[:, -LANES:], rows16[:, :-LANES]], 1)
                at = part * block + b * LANES + a
                chirp_rows[at : at + 16, :] = rows16
    fetches[8].wait()
    for pulse in range(pulses):
        echo_rows[2 * pulse : 2 * pulse + 2, :samples] = echo[0, pulse].astype(F32)
    need = block * (n - 1) + depth
    if need > samples:
        echo_rows[:, samples:] = jnp.zeros((per, echo_rows.shape[1] - samples), F32)
    echo_cat = jnp.concatenate(
        [echo_rows[:, k * block : k * block + depth].astype(BF16) for k in range(n)], 0
    )
    p_ref[: 2 * block, :lanes] = lax.dot_general(
        chirp_rows[...], echo_cat, (((1,), (1,)), ((), ())), preferred_element_type=F32
    )
    odd = (lane_iota(8, lanes)[:1] & 1) == 1
    for at in range(0, block, 32):
        crossed = p_ref[block + at : block + at + 32, :lanes]
        put(
            image_a,
            PAD + at,
            p_ref[at : at + 32, :lanes]
            + jnp.where(odd, -pltpu.roll(crossed, 1, 1), pltpu.roll(crossed, lanes - 1, 1)),
        )

    def shifted(ref, begin, rows, q):
        value = take(ref, PAD + begin, rows)
        if q == 0:
            return value
        keep = (lane_block + q >= 0) & (lane_block + q < n)
        return jnp.where(keep, pltpu.roll(value, (-q * per) % lanes, 1), 0.0)

    src, dst = image_a, image_b
    scratch = (z_ref, x_ref, p_ref, w_ref, table_ref)
    for level in range(local):
        put(src, 0, shifted(src, block - PAD, PAD, -1))
        put(src, PAD + block, shifted(src, 0, PAD, 1))
        merge(level, 2**level, 0, block, src, dst, None, params, *scratch)
        src, dst = dst, src
    pieces = []
    at = -halo
    while at < block + halo:
        q = at // block
        end = min(block + halo, (q + 1) * block)
        pieces.append(shifted(src, at - q * block, end - at, q))
        at = end
    send_ap[...] = jnp.concatenate(pieces, 0).T.reshape(n, per, wide)

    pl.semaphore_wait(barrier, n - 1 + passes - 1)
    copies = []
    for i in range(1, n):
        to = lax.rem(me + i, n)
        copy = pltpu.make_async_remote_copy(
            src_ref=send_ap.at[rev(to)],
            dst_ref=recv_ap.at[me],
            send_sem=send_sem.at[i],
            recv_sem=recv_sem.at[i],
            device_id=(to, my_pass),
            device_id_type=MESH,
        )
        copy.start()
        copies.append(copy)
    recv_ap[me] = send_ap[rev(me)]

    origin = rev(me) * block - halo
    margins = [
        halo if digit + 1 == cross else (digit + 1) * reach // 8 * 8 for digit in range(cross)
    ]
    for digit, margin in enumerate(margins):
        level = local + digit
        prepare(
            level,
            2**level,
            origin + margin,
            (wide - 2 * margin) // 8,
            cells,
            params,
            w_ref,
            table_ref,
        )
    fetches[9].wait()
    bases = invert.shape[1]
    real, imag = invert[0], invert[1]
    table = jnp.concatenate(
        [jnp.concatenate([real, imag], 1), jnp.concatenate([-imag, real], 1)], 0
    ).T
    table_high, table_low = split(table)
    row = row_iota(2 * bases, 2 * passes)
    column = lane_iota(2 * bases, 2 * passes)
    chosen = jnp.zeros((2 * bases, 2 * passes), F32)
    for p in range(passes):
        for c in range(2):
            hit = (column == 2 * p + c) & (row == c * bases + baseline[p])
            chosen = jnp.where(hit, 1.0, chosen)
    chosen = chosen.astype(BF16)
    mixer_high = jnp.dot(table_high, chosen, preferred_element_type=F32).astype(BF16)
    mixer_low = jnp.dot(table_low, chosen, preferred_element_type=F32).astype(BF16)
    mixer[...] = jnp.concatenate([mixer_high, mixer_high, mixer_low], 1)
    put(image_a, 0, blank)
    put(image_b, 0, jnp.zeros((PAD + 24, lanes), F32))
    put(image_a, PAD + wide, blank)
    put(image_b, PAD + wide - 24, jnp.zeros((PAD + 24, lanes), F32))

    for copy in copies:
        copy.wait()
    put(image_a, PAD, recv_ap[...].reshape(lanes, wide).T)

    src, dst = image_a, image_b
    valid = (origin, block, halo, cells)
    for digit, margin in enumerate(margins):
        level = local + digit
        merge(level, 2**level, margin, wide - margin, src, dst, valid, params, *scratch)
        src, dst = dst, src

    beams = 2**levels
    share = beams // passes
    spread = LANES // share
    count = block // spread
    rows = [take(src, PAD + halo + s, count, spread) for s in range(spread)]
    group = lane_iota(8, LANES)[:1] >> (share.bit_length() - 1)
    for chunk in range(lanes // LANES):
        held = [value[:, chunk * LANES : (chunk + 1) * LANES] for value in rows]
        step = spread // 2
        while step:
            upper = (group & step) != 0
            moved = list(held)
            for s in range(spread):
                if s & step == 0:
                    low, high = held[s], held[s + step]
                    moved[s] = jnp.where(upper, pltpu.roll(high, step * share, 1), low)
                    moved[s + step] = jnp.where(
                        upper, high, pltpu.roll(low, LANES - step * share, 1)
                    )
            held = moved
            step //= 2
        for k, value in enumerate(held):
            c, b = divmod(chunk * spread + k, passes)
            send_pass[b, c * count : (c + 1) * count] = value
    copies = []
    for i in range(1, passes):
        to = lax.rem(my_pass + i, passes)
        copy = pltpu.make_async_remote_copy(
            src_ref=send_pass.at[to],
            dst_ref=out.at[my_pass],
            send_sem=send_sem2.at[i],
            recv_sem=recv_sem2.at[i],
            device_id=(me, to),
            device_id_type=MESH,
        )
        copy.start()
        copies.append(copy)
    out[my_pass] = send_pass[my_pass]
    for copy in copies:
        copy.wait()


def power_kernel(passes, count, data, mixer, out, power_ref, out_sem):
    heights = out.shape[0]
    weights = mixer[...]
    chunk = min(count, 8)
    copies = []
    view = power_ref.reshape(heights, count, LANES)
    for k, a0 in enumerate(range(0, count, chunk)):
        values = jnp.concatenate(
            [data[pl.ds(a, 2 * passes, stride=count), :] for a in range(a0, a0 + chunk)], 1
        )
        high = values.astype(BF16).astype(F32)
        low = values - high
        stack = jnp.concatenate([high, low, high], 0).astype(BF16)
        tomo = jnp.dot(weights, stack, preferred_element_type=F32)
        power = tomo[:heights] * tomo[:heights] + tomo[heights:] * tomo[heights:]
        for a in range(chunk):
            power_ref[pl.ds(a0 + a, heights, stride=count), :] = power[
                :, a * LANES : (a + 1) * LANES
            ]
        copy = pltpu.make_async_copy(
            view.at[:, pl.ds(a0, chunk), :], out.at[:, pl.ds(a0, chunk), :], out_sem.at[k]
        )
        copy.start()
        copies.append(copy)
    for copy in copies:
        copy.wait()


def body(
    mesh_shape,
    echo,
    chirp,
    pair_swap,
    range_shift,
    angle_shift,
    range_taps,
    angle_taps,
    phase_rates,
    invert,
    baseline_index,
):
    n, passes = mesh_shape["ap"], mesh_shape["pass"]
    pulses, samples = echo.shape[1], echo.shape[3]
    levels = range_taps.shape[0]
    taps_count = chirp.shape[1]
    cells = samples - taps_count
    block = cells // n
    beams = 2**levels
    share = beams // passes
    heights = invert.shape[1]
    count = block * share // LANES
    lanes = n * 2 * pulses
    reach = RMAX + range_taps.shape[2] // 2
    local = pulses.bit_length() - 1
    wide = up(block + 2 * reach * (levels - local), LANES)
    depth = up(block + taps_count - 1, LANES)
    vmem = pl.BlockSpec(memory_space=pltpu.VMEM)
    hbm = pl.BlockSpec(memory_space=pltpu.HBM)
    operands = (
        echo,
        chirp,
        pair_swap,
        jnp.transpose(range_shift, (0, 2, 1)),
        jnp.transpose(angle_shift, (0, 2, 3, 1)),
        range_taps,
        angle_taps,
        jnp.transpose(phase_rates, (1, 2, 3, 0)),
        jnp.transpose(invert, (0, 2, 1)),
        baseline_index,
    )
    held = [
        (pltpu.VMEM if i in (0, 1, 8) else pltpu.SMEM)(operand.shape, operand.dtype)
        for i, operand in enumerate(operands)
    ]
    stacks, mixer = pl.pallas_call(
        functools.partial(image_kernel, (n, passes, pulses, cells, levels)),
        out_shape=(
            jax.ShapeDtypeStruct((passes, 2 * count, LANES), F32),
            jax.ShapeDtypeStruct((2 * heights, 6 * passes), BF16),
        ),
        in_specs=[hbm] * len(operands),
        out_specs=(vmem, vmem),
        scratch_shapes=held
        + [
            pltpu.VMEM((2 * pulses, up(max(samples, block * (n - 1) + depth), LANES)), F32),
            pltpu.VMEM((2 * block, depth), BF16),
            pltpu.VMEM((lanes // LANES, wide + 2 * PAD, LANES), F32),
            pltpu.VMEM((lanes // LANES, wide + 2 * PAD, LANES), F32),
            pltpu.VMEM((lanes // LANES, wide + 8, LANES), F32),
            pltpu.VMEM((wide, 3 * lanes), BF16),
            pltpu.VMEM((max(wide, 2 * block), 4 * lanes), F32),
            pltpu.VMEM((levels, 3 * lanes, 4 * lanes), BF16),
            pltpu.VMEM((levels, 2, 2, 8 + up(wide // 8, 8), lanes), F32),
            pltpu.VMEM((n, 2 * pulses, wide), F32),
            pltpu.VMEM((n, 2 * pulses, wide), F32),
            pltpu.VMEM((passes, 2 * count, LANES), F32),
            pltpu.SemaphoreType.DMA((len(operands),)),
            pltpu.SemaphoreType.DMA((n,)),
            pltpu.SemaphoreType.DMA((n,)),
            pltpu.SemaphoreType.DMA((passes,)),
            pltpu.SemaphoreType.DMA((passes,)),
        ],
        compiler_params=pltpu.CompilerParams(
            collective_id=0,
            has_side_effects=True,
            vmem_limit_bytes=min(56 * 2**20, 16 * 2**20 + 24 * levels * lanes * lanes),
        ),
        name="image",
    )(*operands)
    power = pl.pallas_call(
        functools.partial(power_kernel, passes, count),
        out_shape=jax.ShapeDtypeStruct((heights, count, LANES), F32),
        in_specs=[vmem, vmem],
        out_specs=hbm,
        scratch_shapes=[
            pltpu.VMEM((heights * count, LANES), F32),
            pltpu.SemaphoreType.DMA((count,)),
        ],
        compiler_params=pltpu.CompilerParams(vmem_limit_bytes=32 * 2**20),
        name="power",
    )(stacks.reshape(passes * 2 * count, LANES), mixer)
    return power.reshape(1, heights, 1, block * share)


def solution(mesh):
    return jax.shard_map(
        functools.partial(body, dict(mesh.shape)),
        mesh=mesh,
        in_specs=(
            P("pass", "ap", None, None),
            P(),
            P("pass", None),
            P("pass", None, None),
            P("pass", None, None, None),
            P(),
            P(),
            P(),
            P(),
            P(),
        ),
        out_specs=P("pass", None, "ap", None),
        check_vma=False,
    )
```

time: 26.1 us -> 26.1 us (level)
  Pallas kernels: 20.7 us -> 19.9 us
  local copies, waits for them, and re-layouts: 4.99 us -> 5.76 us
    pallas_call x1, Pallas kernels: 2.72 us -> 1.95 us  [body(): pl.pallas_call(functools.partial(power_kernel, passes, count), out_shape=...]
    unnamed x20, local copies, waits for them, and re-layouts: 4.99 us -> 5.76 us
where the time goes in v1:
time: 26.1 us; the launch traced here: 25.7 us
  Pallas kernels  19.9 us (76%)
  local copies, waits for them, and re-layouts  5.76 us (22%)
    pallas_call x1, Pallas kernels, body(): pl.pallas_call(functools.partial(image_kernel, (n, passes, pulses, cells,...  18 us
    unnamed x20, local copies, waits for them, and re-layouts  5.76 us
    pallas_call x1, Pallas kernels, body(): pl.pallas_call(functools.partial(power_kernel, passes, count), out_shape=...  1.95 us

profile of v1, /device:TPU:0, one launch (start us, length us, event | category | flops | bytes accessed | tf_op | source)
XLA Modules:
  0.0 25.7 jit_solution(5580543399783569778)
XLA Ops:
  0.0 0.0 copy-start.3
  0.0 0.0 copy-start.7
  0.0 0.0 copy-start.8
  0.0 0.7 %copy-done.3 = f32[6,2,8]{2,1,0:T(2,128)S(1)} copy-done((f32[6,2,8]{2,1,0:T(2,128)S(1)}, f32[6,2,8]{2,1,0:T(2,128)}, u32[]{:S(2)}) %copy-start.3) | copy-done | bytes 408
  0.7 0.0 copy-done.7
  0.7 0.0 copy-done.8
  0.7 0.0 copy-start
  0.7 0.9 %copy-done = bf16[1,8,2,3072]{3,2,1,0:T(2,128)(2,1)S(1)} copy-done((bf16[1,8,2,3072]{3,2,1,0:T(2,128)(2,1)S(1)}, bf16[1,8,2,3072]{3,2,1,0:T(2,128)(2,1)}, u32[]{:S(2)}) %copy-start) | copy-done | bytes 98328
  1.6 0.0 copy-start.1
  1.6 0.8 %copy-done.1 = f32[2,64,32]{1,2,0:T(8,128)S(1)} copy-done((f32[2,64,32]{1,2,0:T(8,128)S(1)}, f32[2,64,32]{1,2,0:T(8,128)}, u32[]{:S(2)}) %copy-start.1) | copy-done | bytes 16408
  2.4 0.0 copy-start.2
  2.4 0.7 %copy-done.2 = f32[6,2,2,8]{3,2,1,0:T(2,128)S(1)} copy-done((f32[6,2,2,8]{3,2,1,0:T(2,128)S(1)}, f32[6,2,2,8]{3,2,1,0:T(2,128)}, u32[]{:S(2)}) %copy-start.2) | copy-done | bytes 792
  3.1 0.0 copy-start.4
  3.1 0.7 %copy-done.4 = bf16[2,1024]{1,0:T(2,128)(2,1)S(1)} copy-done((bf16[2,1024]{1,0:T(2,128)(2,1)S(1)}, bf16[2,1024]{1,0:T(2,128)(2,1)}, u32[]{:S(2)}) %copy-start.4) | copy-done | bytes 4120
  3.7 0.0 copy-start.5
  3.7 0.7 %copy-done.5 = f32[6,2,2,2]{0,3,2,1:T(2,128)S(1)} copy-done((f32[6,2,2,2]{0,3,2,1:T(2,128)S(1)}, f32[6,2,2,2]{0,3,2,1:T(2,128)}, u32[]{:S(2)}) %copy-start.5) | copy-done | bytes 216
  4.4 0.0 copy-start.6
  4.4 0.7 %copy-done.6 = s32[1,6,2,2]{1,3,2,0:T(2,128)S(1)} copy-done((s32[1,6,2,2]{1,3,2,0:T(2,128)S(1)}, s32[1,6,2,2]{1,3,2,0:T(2,128)}, u32[]{:S(2)}) %copy-start.6) | copy-done | bytes 120
  5.1 0.0 copy-start.9
  5.1 0.7 %copy-done.9 = s32[4]{0:T(128)S(1)} copy-done((s32[4]{0:T(128)S(1)}, s32[4]{0:T(128)}, u32[]{:S(2)}) %copy-start.9) | copy-done | bytes 40
  5.8 18.0 %image.1 = (f32[4,64,128]{2,1,0:T(8,128)S(1)}, bf16[128,24]{1,0:T(8,128)(2,1)S(1)}) custom-call(bf16[1,8,2,3072]{3,2,1,0:T(2,128)(2,1)S(1)} %copy-done, bf16[2,1024]{1,0:T(2,128)(2,1)S(1)} %copy-done.4, s32[1,6]{1,0:T(1,128)S(1)} %copy-done.8, s32[1,2,6]{2,1,0:T(2,128)S(1)} %bitcast.10, s32[1,2,2,6]{3,2,1,0:T(2,128)S(1)} %bitcast.9, ...), custom_call_target="tpu_custom_call" | custom-call | tf_op jit(solution)/shard_map/image/pallas_call | solution.py:540
  23.8 2.0 %power.1 = f32[64,32,128]{2,1,0:T(8,128)} custom-call(f32[256,128]{1,0:T(8,128)S(1)} %bitcast.6, bf16[128,24]{1,0:T(8,128)(2,1)S(1)} %get-tuple-element.8.mixer), custom_call_target="tpu_custom_call" | custom-call | tf_op jit(solution)/shard_map/power/pallas_call | solution.py:575
Async XLA Ops:
  0.0 0.7 %copy-start.3 = (f32[6,2,8]{2,1,0:T(2,128)S(1)}, f32[6,2,8]{2,1,0:T(2,128)}, u32[]{:S(2)}) copy-start(f32[6,2,8]{2,1,0:T(2,128)} %range_taps_in.1) | copy-start | bytes 1156
  0.0 0.7 %copy-start.7 = (s32[1,6,2]{1,2,0:T(2,128)S(1)}, s32[1,6,2]{1,2,0:T(2,128)}, u32[]{:S(2)}) copy-start(s32[1,6,2]{1,2,0:T(2,128)} %param.13) | copy-start | bytes 148
  0.0 0.7 %copy-start.8 = (s32[1,6]{1,0:T(1,128)S(1)}, s32[1,6]{1,0:T(1,128)}, u32[]{:S(2)}) copy-start(s32[1,6]{1,0:T(1,128)} %swap_in.1) | copy-start | bytes 76
  0.7 0.9 %copy-start = (bf16[1,8,2,3072]{3,2,1,0:T(2,128)(2,1)S(1)}, bf16[1,8,2,3072]{3,2,1,0:T(2,128)(2,1)}, u32[]{:S(2)}) copy-start(bf16[1,8,2,3072]{3,2,1,0:T(2,128)(2,1)} %echo_in.1) | copy-start | bytes 294916
  1.6 0.8 %copy-start.1 = (f32[2,64,32]{1,2,0:T(8,128)S(1)}, f32[2,64,32]{1,2,0:T(8,128)}, u32[]{:S(2)}) copy-start(f32[2,64,32]{1,2,0:T(8,128)} %param.18) | copy-start | bytes 49156
  2.4 0.7 %copy-start.2 = (f32[6,2,2,8]{3,2,1,0:T(2,128)S(1)}, f32[6,2,2,8]{3,2,1,0:T(2,128)}, u32[]{:S(2)}) copy-start(f32[6,2,2,8]{3,2,1,0:T(2,128)} %angle_taps_in.1) | copy-start | bytes 2308
  3.1 0.7 %copy-start.4 = (bf16[2,1024]{1,0:T(2,128)(2,1)S(1)}, bf16[2,1024]{1,0:T(2,128)(2,1)}, u32[]{:S(2)}) copy-start(bf16[2,1024]{1,0:T(2,128)(2,1)} %chirp_in.1) | copy-start | bytes 12292
  3.7 0.7 %copy-start.5 = (f32[6,2,2,2]{0,3,2,1:T(2,128)S(1)}, f32[6,2,2,2]{0,3,2,1:T(2,128)}, u32[]{:S(2)}) copy-start(f32[6,2,2,2]{0,3,2,1:T(2,128)} %param.17) | copy-start | bytes 580
  4.4 0.7 %copy-start.6 = (s32[1,6,2,2]{1,3,2,0:T(2,128)S(1)}, s32[1,6,2,2]{1,3,2,0:T(2,128)}, u32[]{:S(2)}) copy-start(s32[1,6,2,2]{1,3,2,0:T(2,128)} %param.14) | copy-start | bytes 292
  5.1 0.7 %copy-start.9 = (s32[4]{0:T(128)S(1)}, s32[4]{0:T(128)}, u32[]{:S(2)}) copy-start(s32[4]{0:T(128)} %baseline_in.1) | copy-start | bytes 52

commit v2 on v1

--- a/solution.py
+++ b/solution.py
@@ -571,7 +571,7 @@
             vmem_limit_bytes=min(56 * 2**20, 16 * 2**20 + 24 * levels * lanes * lanes),
         ),
         name="image",
-    )(*operands)
+    )(*[pltpu.with_memory_space_constraint(operand, pltpu.HBM) for operand in operands])
     power = pl.pallas_call(
         functools.partial(power_kernel, passes, count),
         out_shape=jax.ShapeDtypeStruct((heights, count, LANES), F32),

time: 26.1 us -> 20.2 us (0.77); the launches traced: 25.7 us -> 20.1 us
  local copies, waits for them, and re-layouts: 5.76 us -> 0 us
    unnamed x20 -> x0, local copies, waits for them, and re-layouts: 5.76 us -> none
where the time goes in v2:
time: 20.2 us; the launch traced here: 20.1 us
  Pallas kernels  20.1 us (100%)
    pallas_call x1, Pallas kernels, body(): pl.pallas_call(functools.partial(image_kernel, (n, passes, pulses, cells,...  18.1 us
    pallas_call x1, Pallas kernels, body(): pl.pallas_call(functools.partial(power_kernel, passes, count), out_shape=...  1.95 us

profile of v2, /device:TPU:0, one launch (start us, length us, event | category | flops | bytes accessed | tf_op | source)
XLA Modules:
  0.0 20.1 jit_solution(10880436494877009941)
XLA Ops:
  0.0 18.1 %image.1 = (f32[4,64,128]{2,1,0:T(8,128)S(1)}, bf16[128,24]{1,0:T(8,128)(2,1)S(1)}) custom-call(bf16[1,8,2,3072]{3,2,1,0:T(2,128)(2,1)} %echo_in.1, bf16[2,1024]{1,0:T(2,128)(2,1)} %chirp_in.1, s32[1,6]{1,0:T(1,128)} %swap_in.1, s32[1,2,6]{2,1,0:T(2,128)} %bitcast.10, s32[1,2,2,6]{3,2,1,0:T(2,128)} %bitcast.9, f32[6,2,8]{2,1,0:T(2,128)} %range_taps_in.1, ...), custom_call_target="tpu_custom_call" | custom-call | tf_op jit(solution)/shard_map/image/pallas_call | solution.py:540
  18.1 1.9 %power.1 = f32[64,32,128]{2,1,0:T(8,128)} custom-call(f32[256,128]{1,0:T(8,128)S(1)} %bitcast.6, bf16[128,24]{1,0:T(8,128)(2,1)S(1)} %get-tuple-element.8.mixer), custom_call_target="tpu_custom_call" | custom-call | tf_op jit(solution)/shard_map/power/pallas_call | solution.py:575

commit v3 on v2

--- a/solution.py
+++ b/solution.py
@@ -136,7 +136,9 @@
             table_ref[level, c, 1, 8 + 8 * k : 16 + 8 * k] = sine
 
 
-def merge(level, beams, lo, hi, src, dst, valid, params, z_ref, x_ref, p_ref, w_ref, table_ref):
+def merge(
+    level, beams, lo, hi, src, dst, valid, params, z_ref, x_ref, p_ref, w_ref, table_ref, skip=0
+):
     swap_ref, range_shift, _, range_taps, _, _ = params
     lanes = src.shape[0] * LANES
     rows = hi - lo
@@ -167,8 +169,8 @@
     for a in range(rows // 8):
         total = None
         for c in range(2):
-            c_step = table_ref[level, c, 0, 8 + a : 9 + a]
-            s_step = table_ref[level, c, 1, 8 + a : 9 + a]
+            c_step = table_ref[level, c, 0, 8 + skip + a : 9 + skip + a]
+            s_step = table_ref[level, c, 1, 8 + skip + a : 9 + skip + a]
             c_base, s_base = base[c]
             cosine = c_base * c_step - s_base * s_step
             sine = s_base * c_step + c_base * s_step
@@ -416,62 +418,86 @@
 
     src, dst = image_a, image_b
     valid = (origin, block, halo, cells)
-    for digit, margin in enumerate(margins):
+    for digit, margin in enumerate(margins[:-1]):
         level = local + digit
         merge(level, 2**level, margin, wide - margin, src, dst, valid, params, *scratch)
         src, dst = dst, src
 
+    level = levels - 1
     beams = 2**levels
     share = beams // passes
     spread = LANES // share
-    count = block // spread
-    rows = [take(src, PAD + halo + s, count, spread) for s in range(spread)]
+    parts, count = out.shape[0], out.shape[2] // 2
     group = lane_iota(8, LANES)[:1] >> (share.bit_length() - 1)
-    for chunk in range(lanes // LANES):
-        held = [value[:, chunk * LANES : (chunk + 1) * LANES] for value in rows]
-        step = spread // 2
-        while step:
-            upper = (group & step) != 0
-            moved = list(held)
-            for s in range(spread):
-                if s & step == 0:
-                    low, high = held[s], held[s + step]
-                    moved[s] = jnp.where(upper, pltpu.roll(high, step * share, 1), low)
-                    moved[s + step] = jnp.where(
-                        upper, high, pltpu.roll(low, LANES - step * share, 1)
-                    )
-            held = moved
-            step //= 2
-        for k, value in enumerate(held):
-            c, b = divmod(chunk * spread + k, passes)
-            send_pass[b, c * count : (c + 1) * count] = value
     copies = []
-    for i in range(1, passes):
-        to = lax.rem(my_pass + i, passes)
-        copy = pltpu.make_async_remote_copy(
-            src_ref=send_pass.at[to],
-            dst_ref=out.at[my_pass],
-            send_sem=send_sem2.at[i],
-            recv_sem=recv_sem2.at[i],
-            device_id=(me, to),
-            device_id_type=MESH,
-        )
-        copy.start()
-        copies.append(copy)
-    out[my_pass] = send_pass[my_pass]
+    for part in range(parts):
+        lo = halo + part * count * spread
+        merge(
+            level,
+            2**level,
+            lo,
+            lo + count * spread,
+            src,
+            dst,
+            valid,
+            params,
+            *scratch,
+            skip=part * count * spread // 8,
+        )
+        rows = [take(dst, PAD + lo + s, count, spread) for s in range(spread)]
+        for chunk in range(lanes // LANES):
+            held = [value[:, chunk * LANES : (chunk + 1) * LANES] for value in rows]
+            step = spread // 2
+            while step:
+                upper = (group & step) != 0
+                moved = list(held)
+                for s in range(spread):
+                    if s & step == 0:
+                        low, high = held[s], held[s + step]
+                        moved[s] = jnp.where(upper, pltpu.roll(high, step * share, 1), low)
+                        moved[s + step] = jnp.where(
+                            upper, high, pltpu.roll(low, LANES - step * share, 1)
+                        )
+                held = moved
+                step //= 2
+            for k, value in enumerate(held):
+                c, b = divmod(chunk * spread + k, passes)
+                send_pass[part, b, c * count : (c + 1) * count] = value
+        for i in range(1, passes):
+            to = lax.rem(my_pass + i, passes)
+            copy = pltpu.make_async_remote_copy(
+                src_ref=send_pass.at[part, to],
+                dst_ref=out.at[part, my_pass],
+                send_sem=send_sem2.at[part * passes + i],
+                recv_sem=recv_sem2.at[part * passes + i],
+                device_id=(me, to),
+                device_id_type=MESH,
+            )
+            copy.start()
+            copies.append(copy)
+        out[part, my_pass] = send_pass[part, my_pass]
     for copy in copies:
         copy.wait()
 
 
-def power_kernel(passes, count, data, mixer, out, power_ref, out_sem):
-    heights = out.shape[0]
+def power_kernel(passes, parts, data, mixer, out, power_ref, out_sem):
+    heights, count = out.shape[:2]
+    within = count // parts
+    pitch = power_ref.shape[0] // heights
     weights = mixer[...]
     chunk = min(count, 8)
     copies = []
-    view = power_ref.reshape(heights, count, LANES)
+    view = power_ref.reshape(heights, pitch, LANES)
     for k, a0 in enumerate(range(0, count, chunk)):
         values = jnp.concatenate(
-            [data[pl.ds(a, 2 * passes, stride=count), :] for a in range(a0, a0 + chunk)], 1
+            [
+                data[
+                    pl.ds(a // within * within * 2 * passes + a % within, 2 * passes, stride=within),
+                    :,
+                ]
+                for a in range(a0, a0 + chunk)
+            ],
+            1,
         )
         high = values.astype(BF16).astype(F32)
         low = values - high
@@ -479,7 +505,7 @@
         tomo = jnp.dot(weights, stack, preferred_element_type=F32)
         power = tomo[:heights] * tomo[:heights] + tomo[heights:] * tomo[heights:]
         for a in range(chunk):
-            power_ref[pl.ds(a0 + a, heights, stride=count), :] = power[
+            power_ref[pl.ds(a0 + a, heights, stride=pitch), :] = power[
                 :, a * LANES : (a + 1) * LANES
             ]
         copy = pltpu.make_async_copy(
@@ -514,6 +540,7 @@
     share = beams // passes
     heights = invert.shape[1]
     count = block * share // LANES
+    parts = 2 if count % 16 == 0 else 1
     lanes = n * 2 * pulses
     reach = RMAX + range_taps.shape[2] // 2
     local = pulses.bit_length() - 1
@@ -540,7 +567,7 @@
     stacks, mixer = pl.pallas_call(
         functools.partial(image_kernel, (n, passes, pulses, cells, levels)),
         out_shape=(
-            jax.ShapeDtypeStruct((passes, 2 * count, LANES), F32),
+            jax.ShapeDtypeStruct((parts, passes, 2 * count // parts, LANES), F32),
             jax.ShapeDtypeStruct((2 * heights, 6 * passes), BF16),
         ),
         in_specs=[hbm] * len(operands),
@@ -558,12 +585,12 @@
             pltpu.VMEM((levels, 2, 2, 8 + up(wide // 8, 8), lanes), F32),
             pltpu.VMEM((n, 2 * pulses, wide), F32),
             pltpu.VMEM((n, 2 * pulses, wide), F32),
-            pltpu.VMEM((passes, 2 * count, LANES), F32),
+            pltpu.VMEM((parts, passes, 2 * count // parts, LANES), F32),
             pltpu.SemaphoreType.DMA((len(operands),)),
             pltpu.SemaphoreType.DMA((n,)),
             pltpu.SemaphoreType.DMA((n,)),
-            pltpu.SemaphoreType.DMA((passes,)),
-            pltpu.SemaphoreType.DMA((passes,)),
+            pltpu.SemaphoreType.DMA((parts * passes,)),
+            pltpu.SemaphoreType.DMA((parts * passes,)),
         ],
         compiler_params=pltpu.CompilerParams(
             collective_id=0,
@@ -573,12 +600,12 @@
         name="image",
     )(*[pltpu.with_memory_space_constraint(operand, pltpu.HBM) for operand in operands])
     power = pl.pallas_call(
-        functools.partial(power_kernel, passes, count),
+        functools.partial(power_kernel, passes, parts),
         out_shape=jax.ShapeDtypeStruct((heights, count, LANES), F32),
         in_specs=[vmem, vmem],
         out_specs=hbm,
         scratch_shapes=[
-            pltpu.VMEM((heights * count, LANES), F32),
+            pltpu.VMEM((heights * (count + 8), LANES), F32),
             pltpu.SemaphoreType.DMA((count,)),
         ],
         compiler_params=pltpu.CompilerParams(vmem_limit_bytes=32 * 2**20),

time: 20.2 us -> 20.4 us (level)
    pallas_call x1, Pallas kernels: 18.1 us -> 18.8 us  [body(): pl.pallas_call(functools.partial(image_kernel, (n, passes, pulses, cells,...]
    pallas_call x1, Pallas kernels: 1.95 us -> 1.47 us  [body(): pl.pallas_call(functools.partial(power_kernel, passes, parts), out_shape=...]
where the time goes in v3:
time: 20.4 us; the launch traced here: 20.2 us
  Pallas kernels  20.2 us (99%)
    pallas_call x1, Pallas kernels, body(): pl.pallas_call(functools.partial(image_kernel, (n, passes, pulses, cells,...  18.8 us
    pallas_call x1, Pallas kernels, body(): pl.pallas_call(functools.partial(power_kernel, passes, parts), out_shape=...  1.47 us

profile of v3, /device:TPU:0, one launch (start us, length us, event | category | flops | bytes accessed | tf_op | source)
XLA Modules:
  0.0 20.2 jit_solution(3587941220979964916)
XLA Ops:
  0.0 18.8 %image.1 = (f32[2,4,32,128]{3,2,1,0:T(8,128)S(1)}, bf16[128,24]{1,0:T(8,128)(2,1)S(1)}) custom-call(bf16[1,8,2,3072]{3,2,1,0:T(2,128)(2,1)} %echo_in.1, bf16[2,1024]{1,0:T(2,128)(2,1)} %chirp_in.1, s32[1,6]{1,0:T(1,128)} %swap_in.1, s32[1,2,6]{2,1,0:T(2,128)} %bitcast.10, s32[1,2,2,6]{3,2,1,0:T(2,128)} %bitcast.9, f32[6,2,8]{2,1,0:T(2,128)} %range_taps_in.1, ...), custom_call_target="tpu_custom_call" | custom-call | tf_op jit(solution)/shard_map/image/pallas_call | solution.py:567
  18.8 1.5 %power.1 = f32[64,32,128]{2,1,0:T(8,128)} custom-call(f32[256,128]{1,0:T(8,128)S(1)} %bitcast.6, bf16[128,24]{1,0:T(8,128)(2,1)S(1)} %get-tuple-element.8.mixer), custom_call_target="tpu_custom_call" | custom-call | tf_op jit(solution)/shard_map/power/pallas_call | solution.py:602
